TPU v7x, 32 devices: a whole 2x2x4 slice. The times are simulated.
32 devices in a mesh: pages: 8 (over z, y), heads: 4 (over x, core).
Axes of the slice: x: 2, y: 2, z: 4, core: 2. Of those that a mesh axis runs over, the one named last changes fastest.
Arguments:
- tokens: bfloat16 [32, 561, 768], P(('pages', 'heads')), may hold values from -6 to 6
- w_qkv: bfloat16 [768, 3, 768], P(None, None, 'heads'), may hold values from -0.21875 to 0.21875
- qv_bias: float32 [2, 768], P(None, 'heads'), may hold values from -0.625 to 0.625
- w_out: bfloat16 [768, 768], P('heads'), may hold values from -2 to 2
- out_bias: float32 [768], replicated, may hold values from -1.75 to 1.75
- norm1_gain: float32 [768], replicated, may hold values from 0.5 to 1.5
- norm1_shift: float32 [768], replicated, may hold values from -1.75 to 1.75
- w_up: bfloat16 [768, 3072], P(None, 'heads'), may hold values from -0.21875 to 0.21875
- up_bias: bfloat16 [3072], P('heads'), may hold values from -1.75 to 1.75
- w_down: bfloat16 [3072, 768], P('heads'), may hold values from -0.109375 to 0.109375
- down_bias: float32 [768], replicated, may hold values from -1.75 to 1.75
- norm2_gain: float32 [768], replicated, may hold values from 0.5 to 1.5
- norm2_shift: float32 [768], replicated, may hold values from -1.75 to 1.75
- pos_table: float32 [12, 32], P('heads'), may hold values from -3 to 3
- box_table: float32 [2, 12, 64], P(None, 'heads'), may hold values from -3 to 3
- receipt_lengths: int32 [32, 8], P('pages'), may hold values from 1 to 128, 512 in all within a row
- page_boxes: int32 [32, 2, 561], P('pages'), may hold values from 0 to 1000
- out_cotangent: bfloat16 [32, 561, 768], P(('pages', 'heads')), may hold values from -6 to 6
Outputs:
- layer_out: bfloat16 [32, 561, 768], P(('pages', 'heads'))
- grad_tokens: bfloat16 [32, 561, 768], P(('pages', 'heads'))
- grad_w_qkv: float32 [768, 3, 768], P('pages', None, 'heads')
- grad_qv_bias: float32 [2, 768], P(None, 'heads')
- grad_w_out: float32 [768, 768], P('heads', 'pages')
- grad_out_bias: float32 [768], replicated
- grad_norm1_gain: float32 [768], replicated
- grad_norm1_shift: float32 [768], replicated
- grad_w_up: float32 [768, 3072], P('pages', 'heads')
- grad_up_bias: float32 [3072], P('heads')
- grad_w_down: float32 [3072, 768], P('heads', 'pages')
- grad_down_bias: float32 [768], replicated
- grad_norm2_gain: float32 [768], replicated
- grad_norm2_shift: float32 [768], replicated
- grad_pos_table: float32 [12, 32], P('heads')
- grad_box_table: float32 [2, 12, 64], P(None, 'heads')
Inputs may be any that keep to these rules, and one draw needn't show every extreme that they name: `receipt_lengths`: each page's 8 receipt lengths sum to 512.
All inputs are finite; a program needn't handle non-finite values.
Results may differ from a plain program's by a relative error of at most 0.02.
Values may be sent and summed in bfloat16 or wider, within the bound.
No kernel may reach another device: no remote copies, remote signals or barrier semaphores. Data moves between devices by JAX's collectives and lax.ppermute only.
A program may use at most 256 MiB of HBM per device.

v0:
```python
import math

import jax
import jax.numpy as jnp
import numpy as np
from jax import lax
from jax.sharding import PartitionSpec as P

HEAD_DIM = 64
TEXT = 512
NB1 = 32
MD1 = 128
NB2 = 64
MD2 = 256
LEN = 561


EPSILON = 1e-05
MASKED_SCORE = -1e30


def thresholds(buckets, max_reach):
    half_range = buckets // 2
    exact_range = half_range // 2
    levels = half_range - exact_range
    return np.array(
        [
            math.ceil(exact_range * (max_reach / exact_range) ** (step_index / levels) - 1e-09)
            for step_index in range(1, levels)
        ],
        dtype=np.int32,
    )


def bucketed(offsets, buckets, max_reach):
    half_range = buckets // 2
    exact_range = half_range // 2
    distance = jnp.abs(offsets)
    bounds = jnp.asarray(thresholds(buckets, max_reach), dtype=jnp.int32)
    passed = jnp.sum((distance[..., None] >= bounds).astype(jnp.int32), axis=-1, dtype=jnp.int32)
    inside = jnp.where(distance < exact_range, distance, exact_range + passed)
    return jnp.where(offsets > 0, half_range, 0).astype(jnp.int32) + inside


def page_masks(lengths, page_boxes):
    receipt_ends = jnp.cumsum(lengths, dtype=jnp.int32)
    positions = jnp.arange(LEN, dtype=jnp.int32)
    segment = jnp.sum(
        (positions[:, None] >= receipt_ends[None, :]).astype(jnp.int32), axis=1, dtype=jnp.int32
    )
    visual = positions >= TEXT
    allowed = (segment[:, None] == segment[None, :]) | visual[:, None] | visual[None, :]
    pos_ids = bucketed(positions[None, :] - positions[:, None], NB1, MD1)
    x_ids = bucketed(page_boxes[0][None, :] - page_boxes[0][:, None], NB2, MD2)
    y_ids = bucketed(page_boxes[1][None, :] - page_boxes[1][:, None], NB2, MD2)
    return (allowed, pos_ids, x_ids, y_ids)


def hot_mask(bucket_ids, count):
    return (bucket_ids[..., None] == jnp.arange(count, dtype=jnp.int32)).astype(jnp.bfloat16)


def split_pair(values):
    high_part = values.astype(jnp.bfloat16)
    rest_part = (values - high_part.astype(jnp.float32)).astype(jnp.bfloat16)
    return (high_part, rest_part)


def table_bias(table, bucket_ids):
    count = table.shape[1]
    heads_here = table.shape[0]
    high_part, rest_part = split_pair(table)
    both = jnp.concatenate((high_part, rest_part), axis=0)
    summed = jnp.einsum(
        "qkb,hb->hqk", hot_mask(bucket_ids, count), both, preferred_element_type=jnp.float32
    )
    return summed[:heads_here] + summed[heads_here:]


def table_grad(d_scores, bucket_ids, count):
    heads_here = d_scores.shape[0]
    high_part, rest_part = split_pair(d_scores)
    both = jnp.concatenate((high_part, rest_part), axis=0)
    summed = jnp.einsum(
        "hqk,qkb->hb", both, hot_mask(bucket_ids, count), preferred_element_type=jnp.float32
    )
    return summed[:heads_here] + summed[heads_here:]


def lookup_hot(pos_table, box_table, pos_ids, x_ids, y_ids):
    return (
        table_bias(pos_table, pos_ids)
        + table_bias(box_table[0], x_ids)
        + table_bias(box_table[1], y_ids)
    )


def layer_norm(values, gain_vec, shift_vec):
    centered = values - jnp.mean(values, axis=-1, keepdims=True)
    inv_std = lax.rsqrt(jnp.mean(centered * centered, axis=-1, keepdims=True) + EPSILON)
    return centered * inv_std * gain_vec + shift_vec


def exact_gelu(values):
    return jax.nn.gelu(values, approximate=False)


def contract(left_mat, right_mat, left_dim, right_dim):
    return lax.dot_general(
        left_mat,
        right_mat,
        (((left_dim,), (right_dim,)), ((), ())),
        preferred_element_type=jnp.float32,
    )


def page_scores(page_q, page_k, allowed, biases):
    raw_scores = jnp.einsum("qhd,khd->hqk", page_q, page_k, preferred_element_type=jnp.float32) * (
        1.0 / math.sqrt(HEAD_DIM)
    )
    return jnp.where(allowed[None], raw_scores + biases, MASKED_SCORE)


def on_device(
    tokens,
    w_qkv,
    qv_bias,
    w_out,
    out_bias,
    norm1_gain,
    norm1_shift,
    w_up,
    up_bias,
    w_down,
    down_bias,
    norm2_gain,
    norm2_shift,
    pos_table,
    box_table,
    receipt_lengths,
    page_boxes,
    out_cotangent,
):
    seq_len = tokens.shape[1]
    model_width = tokens.shape[2]
    local_rows = tokens.shape[0] * seq_len
    heads_here = pos_table.shape[0]
    inner_width = heads_here * HEAD_DIM
    group_pages = receipt_lengths.shape[0]
    pos_count = pos_table.shape[1]
    box_count = box_table.shape[2]
    qkv_matrix = w_qkv.reshape(model_width, 3 * inner_width)
    page_ids = lax.map(
        lambda page_pair: page_masks(page_pair[0], page_pair[1]), (receipt_lengths, page_boxes)
    )

    def run_forward():
        gathered = lax.all_gather(tokens, "heads", axis=0, tiled=True)
        mixed_proj = jnp.dot(
            gathered.reshape(-1, model_width), qkv_matrix, preferred_element_type=jnp.float32
        )
        mixed_proj = mixed_proj.reshape(group_pages, seq_len, 3, heads_here, HEAD_DIM)
        queries = (mixed_proj[:, :, 0] + qv_bias[0].reshape(heads_here, HEAD_DIM)).astype(
            jnp.bfloat16
        )
        keys_low = mixed_proj[:, :, 1].astype(jnp.bfloat16)
        values = (mixed_proj[:, :, 2] + qv_bias[1].reshape(heads_here, HEAD_DIM)).astype(
            jnp.bfloat16
        )

        def page_attention(page_items):
            page_q, page_k, page_v, allowed, pos_ids, x_ids, y_ids = page_items
            scores = page_scores(
                page_q, page_k, allowed, lookup_hot(pos_table, box_table, pos_ids, x_ids, y_ids)
            )
            row_max = jnp.max(scores, axis=-1, keepdims=True)
            exponent = jnp.exp(scores - row_max)
            row_total = jnp.sum(exponent, axis=-1, keepdims=True)
            attn_weights = (exponent / row_total).astype(jnp.bfloat16)
            page_out = jnp.einsum(
                "hqk,khd->qhd", attn_weights, page_v, preferred_element_type=jnp.float32
            )
            return (page_out, row_max[..., 0] + jnp.log(row_total[..., 0]))

        attended, log_total = lax.map(page_attention, (queries, keys_low, values) + page_ids)
        attended = attended.reshape(-1, inner_width).astype(jnp.bfloat16)
        projected = lax.psum_scatter(
            jnp.dot(attended, w_out, preferred_element_type=jnp.float32).astype(jnp.bfloat16),
            "heads",
            scatter_dimension=0,
            tiled=True,
        ).astype(jnp.float32)
        first_in = (
            projected + out_bias + tokens.reshape(local_rows, model_width).astype(jnp.float32)
        )
        first_out = layer_norm(first_in, norm1_gain, norm1_shift)
        first_low = first_out.astype(jnp.bfloat16)
        mid_rows = lax.all_gather(first_low, "heads", axis=0, tiled=True)
        up_proj = jnp.dot(mid_rows, w_up, preferred_element_type=jnp.float32) + up_bias.astype(
            jnp.float32
        )
        hidden = exact_gelu(up_proj).astype(jnp.bfloat16)
        ffn_out = lax.psum_scatter(
            jnp.dot(hidden, w_down, preferred_element_type=jnp.float32).astype(jnp.bfloat16),
            "heads",
            scatter_dimension=0,
            tiled=True,
        ).astype(jnp.float32)
        ffn_mats = (w_up, w_down)
        second_in = ffn_out + down_bias + first_out
        return (
            gathered,
            queries,
            keys_low,
            values,
            log_total,
            attended,
            first_in,
            mid_rows,
            up_proj,
            hidden,
            ffn_mats,
            second_in,
        )

    forward_state = run_forward()
    layer_out = (
        layer_norm(forward_state[11], norm2_gain, norm2_shift)
        .astype(jnp.bfloat16)
        .reshape(tokens.shape)
    )
    (
        gathered,
        queries,
        keys_low,
        values,
        log_total,
        attended,
        first_in,
        mid_rows,
        up_proj,
        hidden,
        ffn_mats,
        second_in,
    ) = run_forward()
    _, second_pull = jax.vjp(layer_norm, second_in, norm2_gain, norm2_shift)
    d_second, g_gain2, g_shift2 = second_pull(
        out_cotangent.reshape(local_rows, model_width).astype(jnp.float32)
    )
    g_down_bias = jnp.sum(d_second, axis=0)
    d_ffn_low = d_second.astype(jnp.bfloat16)
    _, gelu_pull = jax.vjp(exact_gelu, up_proj)
    d_ffn_all = lax.all_gather(d_ffn_low, "heads", axis=0, tiled=True)
    d_hidden = contract(d_ffn_all, w_down, 1, 1)
    d_up_low = gelu_pull(d_hidden)[0].astype(jnp.bfloat16)
    g_w_up = contract(mid_rows, d_up_low, 0, 0)
    g_up_bias = jnp.sum(d_up_low, axis=0, dtype=jnp.float32)
    g_w_down = contract(hidden, d_ffn_all, 0, 0)
    d_mid = lax.psum_scatter(
        contract(d_up_low, w_up, 1, 1).astype(jnp.bfloat16),
        "heads",
        scatter_dimension=0,
        tiled=True,
    ).astype(jnp.float32)
    _, first_pull = jax.vjp(layer_norm, first_in, norm1_gain, norm1_shift)
    d_first, g_gain1, g_shift1 = first_pull(d_second + d_mid)
    g_out_bias = jnp.sum(d_first, axis=0)
    d_proj_all = lax.all_gather(d_first.astype(jnp.bfloat16), "heads", axis=0, tiled=True)
    g_w_out = contract(attended, d_proj_all, 0, 0)
    d_attended = (
        contract(d_proj_all, w_out, 1, 1)
        .astype(jnp.bfloat16)
        .reshape(group_pages, seq_len, heads_here, HEAD_DIM)
    )

    def page_backward(page_items):
        page_q, page_k, page_v, page_lse, page_grad, allowed, pos_ids, x_ids, y_ids = page_items
        biases = lookup_hot(pos_table, box_table, pos_ids, x_ids, y_ids)
        scores = page_scores(page_q, page_k, allowed, biases)
        attn_probs = jnp.exp(scores - page_lse[..., None])
        probs_low = attn_probs.astype(jnp.bfloat16)
        d_values = jnp.einsum(
            "hqk,qhd->khd", probs_low, page_grad, preferred_element_type=jnp.float32
        )
        d_probs = jnp.einsum("qhd,khd->hqk", page_grad, page_v, preferred_element_type=jnp.float32)
        d_scores = attn_probs * (d_probs - jnp.sum(attn_probs * d_probs, axis=-1, keepdims=True))
        g_pos_page = table_grad(d_scores, pos_ids, pos_count)
        g_box_page = jnp.stack(
            (table_grad(d_scores, x_ids, box_count), table_grad(d_scores, y_ids, box_count))
        )
        d_raw = d_scores.astype(jnp.bfloat16)
        scale_factor = 1.0 / math.sqrt(HEAD_DIM)
        d_queries = (
            jnp.einsum("hqk,khd->qhd", d_raw, page_k, preferred_element_type=jnp.float32)
            * scale_factor
        )
        d_keys = (
            jnp.einsum("hqk,qhd->khd", d_raw, page_q, preferred_element_type=jnp.float32)
            * scale_factor
        )
        return (
            jnp.stack((d_queries, d_keys, d_values), axis=1).astype(jnp.bfloat16),
            g_pos_page,
            g_box_page,
        )

    d_mixed, g_pos_pages, g_box_pages = lax.map(
        page_backward, (queries, keys_low, values, log_total, d_attended) + page_ids
    )
    d_mixed = d_mixed.reshape(-1, 3 * inner_width)
    g_w_qkv = contract(gathered.reshape(-1, model_width), d_mixed, 0, 0).reshape(
        model_width, 3, inner_width
    )
    bias_grads = jnp.sum(d_mixed.reshape(-1, 3, inner_width), axis=0, dtype=jnp.float32)
    g_qv_bias = jnp.stack((bias_grads[0], bias_grads[2]))
    d_inputs = lax.psum_scatter(
        contract(d_mixed, qkv_matrix, 1, 1).astype(jnp.bfloat16),
        "heads",
        scatter_dimension=0,
        tiled=True,
    ).astype(jnp.float32)
    grad_tokens = (d_inputs + d_first).astype(jnp.bfloat16).reshape(tokens.shape)
    matrix_sums = (
        lax.psum_scatter(g_w_qkv, "pages", scatter_dimension=0, tiled=True),
        lax.psum_scatter(g_w_out, "pages", scatter_dimension=1, tiled=True),
        lax.psum_scatter(g_w_up, "pages", scatter_dimension=0, tiled=True),
        lax.psum_scatter(g_w_down, "pages", scatter_dimension=1, tiled=True),
    )
    small_sums = lax.psum(
        (g_qv_bias, g_up_bias, jnp.sum(g_pos_pages, axis=0), jnp.sum(g_box_pages, axis=0)), "pages"
    )
    shared_sums = lax.psum(
        (g_out_bias, g_gain1, g_shift1, g_down_bias, g_gain2, g_shift2), ("pages", "heads")
    )
    return (
        layer_out,
        grad_tokens,
        matrix_sums[0],
        small_sums[0],
        matrix_sums[1],
        shared_sums[0],
        shared_sums[1],
        shared_sums[2],
        matrix_sums[2],
        small_sums[1],
        matrix_sums[3],
        shared_sums[3],
        shared_sums[4],
        shared_sums[5],
        small_sums[2],
        small_sums[3],
    )


def solution(mesh):
    placed = (
        P(("pages", "heads"), None, None),
        P(None, None, "heads"),
        P(None, "heads"),
        P("heads", None),
        P(),
        P(),
        P(),
        P(None, "heads"),
        P("heads"),
        P("heads", None),
        P(),
        P(),
        P(),
        P("heads", None),
        P(None, "heads", None),
        P("pages", None),
        P("pages", None, None),
        P(("pages", "heads"), None, None),
    )
    return jax.shard_map(
        on_device,
        mesh=mesh,
        in_specs=placed,
        out_specs=(
            P(("pages", "heads"), None, None),
            P(("pages", "heads"), None, None),
            P("pages", None, "heads"),
            P(None, "heads"),
            P("heads", "pages"),
            P(),
            P(),
            P(),
            P("pages", "heads"),
            P("heads"),
            P("heads", "pages"),
            P(),
            P(),
            P(),
            P("heads", None),
            P(None, "heads", None),
        ),
        check_vma=False,
    )
```

profile of v0, /device:TPU:0, one launch (start us, length us, event | category | flops | bytes accessed | tf_op | source)
XLA Modules:
  0.0 4918.5 jit_solution(17199853623068229723)
XLA Ops:
  8.0 56.9 %while.60 = (s32[]{:T(128)}, pred[4,561,561]{1,2,0:T(8,128)(4,1)S(1)}, s32[4,561,561]{2,1,0:T(8,128)}, s32[4,561,561]{2,1,0:T(8,128)}, s32[4,561,561]{2,1,0:T(8,...) while((s32[]{:T(128)}, ...), condition=%wide.region_6.7_spmd.clone.clone, body=%wide.region_0.6_spmd.sunk.clone.clone.sunk | while | flops 44389184 | bytes 21762656 | solution.py:153
  73.7 489.7 %while.58 = (s32[]{:T(128)}, bf16[4,561,3,64]{1,3,2,0:T(8,128)(2,1)}, f32[4,3,561]{2,1,0:T(4,128)}, bf16[4,561,3,64]{1,3,2,0:T(8,128)(2,1)}, pred[4,561,561]{1,2...) while((s32[]{:T(128)}, ...), condition=%wide.region_20.21_spmd, body=%wide.region_17.20_spmd.sunk | while | flops 909547264 | bytes 174442864 | solution.py:185
  92.3 13.7 fusion.340
  570.1 507.0 %while.57 = (s32[]{:T(128)}, bf16[4,561,3,64]{1,3,2,0:T(8,128)(2,1)}, bf16[4,561,3,64]{1,3,2,0:T(8,128)(2,1)}, pred[4,561,561]{1,2,0:T(8,128)(4,1)S(1)}, bf16[4,...) while((s32[]{:T(128)}, ...), condition=%wide.region_10.11_spmd, body=%wide.region_7.10_spmd.sunk | while | flops 908607616 | bytes 194452880 | solution.py:185
  1090.4 64.7 %fusion.210 = (bf16[568,768]{1,0:T(8,128)(2,1)}, bf16[568,768]{1,0:T(8,128)(2,1)S(1)}) fusion(bf16[2244,768]{1,0:T(8,128)(2,1)} %convolution_convert_fusion.1, bf16[2244,768]{1,0:T(8,128)(2,1)} %convolution_convert_fusion.2), kind=kCustom, calls=%all-reduce-scatter.7 | all-reduce-scatter fusion | flops 3489793 | bytes 8638976
  1177.8 30.9 all-gather.14.cloned.1.call-done
  1213.4 20.2 multiply_convert_fusion
  1239.6 35.0 fusion.3
  1290.6 34.6 all-gather.16.cloned.1.call-done
  1348.0 34.9 fusion.4
  1402.3 34.2 all-gather.18.cloned.1.call-done
  1466.7 40.5 all-reduce.12
  1512.6 3219.7 %while.59 = (s32[]{:T(128)}, bf16[4,561,3,3,64]{1,4,3,2,0:T(8,128)(2,1)}, f32[4,3,32]{2,1,0:T(4,128)}, f32[4,2,3,64]{3,2,1,0:T(4,128)}, bf16[4,561,3,64]{1,3,2,0...) while((s32[]{:T(128)}, ...), condition=%wide.region_34.35_spmd, body=%wide.region_32.34_spmd.sunk | while | flops 1934868608 | bytes 457105568 | solution.py:307
  1518.8 15.4 iota_compare_fusion.42
  1534.3 229.4 %copy.301 = pred[561,561,64]{1,2,0:T(32,128)(4,1)} copy(pred[561,561,64]{0,2,1:T(32,128)(4,1)} %iota_compare_fusion.42) | data formatting | bytes 40284288 | tf_op jit(solution)/shard_map/while/body/eval_jaxpr/eq | solution.py:60
  1800.7 15.4 iota_compare_fusion.43
  1816.2 229.4 %copy.305 = pred[561,561,64]{1,2,0:T(32,128)(4,1)} copy(pred[561,561,64]{0,2,1:T(32,128)(4,1)} %iota_compare_fusion.43) | data formatting | bytes 40284288 | tf_op jit(solution)/shard_map/while/body/eval_jaxpr/eq | solution.py:60
  2093.3 115.5 %copy.309 = pred[561,561,32]{1,2,0:T(32,128)(4,1)} copy(pred[561,561,32]{0,2,1:T(32,128)(4,1)} %iota_compare_fusion.44) | data formatting | bytes 20142144 | tf_op jit(solution)/shard_map/while/body/eval_jaxpr/eq | solution.py:60
  2221.4 14.7 fusion.370
  2268.9 14.6 fusion.376
  2283.5 14.8 fusion.375
  2322.2 15.4 iota_compare_fusion.42
  2337.6 229.4 %copy.301 = pred[561,561,64]{1,2,0:T(32,128)(4,1)} copy(pred[561,561,64]{0,2,1:T(32,128)(4,1)} %iota_compare_fusion.42) | data formatting | bytes 40284288 | tf_op jit(solution)/shard_map/while/body/eval_jaxpr/eq | solution.py:60
  2604.0 15.4 iota_compare_fusion.43
  2619.4 229.4 %copy.305 = pred[561,561,64]{1,2,0:T(32,128)(4,1)} copy(pred[561,561,64]{0,2,1:T(32,128)(4,1)} %iota_compare_fusion.43) | data formatting | bytes 40284288 | tf_op jit(solution)/shard_map/while/body/eval_jaxpr/eq | solution.py:60
  2896.4 115.5 %copy.309 = pred[561,561,32]{1,2,0:T(32,128)(4,1)} copy(pred[561,561,32]{0,2,1:T(32,128)(4,1)} %iota_compare_fusion.44) | data formatting | bytes 20142144 | tf_op jit(solution)/shard_map/while/body/eval_jaxpr/eq | solution.py:60
  3024.5 14.9 fusion.370
  3072.2 14.6 fusion.376
  3086.9 14.8 fusion.375
  3125.2 15.4 iota_compare_fusion.42
  3140.6 229.4 %copy.301 = pred[561,561,64]{1,2,0:T(32,128)(4,1)} copy(pred[561,561,64]{0,2,1:T(32,128)(4,1)} %iota_compare_fusion.42) | data formatting | bytes 40284288 | tf_op jit(solution)/shard_map/while/body/eval_jaxpr/eq | solution.py:60
  3407.3 15.4 iota_compare_fusion.43
  3422.7 229.4 %copy.305 = pred[561,561,64]{1,2,0:T(32,128)(4,1)} copy(pred[561,561,64]{0,2,1:T(32,128)(4,1)} %iota_compare_fusion.43) | data formatting | bytes 40284288 | tf_op jit(solution)/shard_map/while/body/eval_jaxpr/eq | solution.py:60
  3699.7 115.5 %copy.309 = pred[561,561,32]{1,2,0:T(32,128)(4,1)} copy(pred[561,561,32]{0,2,1:T(32,128)(4,1)} %iota_compare_fusion.44) | data formatting | bytes 20142144 | tf_op jit(solution)/shard_map/while/body/eval_jaxpr/eq | solution.py:60
  3827.7 14.7 fusion.370
  3875.3 14.6 fusion.376
  3889.9 15.0 fusion.375
  3928.4 15.4 iota_compare_fusion.42
  3943.9 229.4 %copy.301 = pred[561,561,64]{1,2,0:T(32,128)(4,1)} copy(pred[561,561,64]{0,2,1:T(32,128)(4,1)} %iota_compare_fusion.42) | data formatting | bytes 40284288 | tf_op jit(solution)/shard_map/while/body/eval_jaxpr/eq | solution.py:60
  4210.3 15.4 iota_compare_fusion.43
  4225.8 229.4 %copy.305 = pred[561,561,64]{1,2,0:T(32,128)(4,1)} copy(pred[561,561,64]{0,2,1:T(32,128)(4,1)} %iota_compare_fusion.43) | data formatting | bytes 40284288 | tf_op jit(solution)/shard_map/while/body/eval_jaxpr/eq | solution.py:60
  4502.9 115.5 %copy.309 = pred[561,561,32]{1,2,0:T(32,128)(4,1)} copy(pred[561,561,32]{0,2,1:T(32,128)(4,1)} %iota_compare_fusion.44) | data formatting | bytes 20142144 | tf_op jit(solution)/shard_map/while/body/eval_jaxpr/eq | solution.py:60
  4631.0 14.7 fusion.370
  4678.5 14.6 fusion.376
  4693.2 14.8 fusion.375
  4762.0 22.4 convolution_convert_fusion.5
  4784.6 64.4 %fusion.209 = (bf16[568,768]{1,0:T(8,128)(2,1)}, bf16[568,768]{1,0:T(8,128)(2,1)}) fusion(bf16[2244,768]{1,0:T(8,128)(2,1)} %convolution_convert_fusion.5, bf16[2244,768]{1,0:T(8,128)(2,1)} %convolution_convert_fusion), kind=kCustom, calls=%all-reduce-scatter.6 | all-reduce-scatter fusion | flops 3489793 | bytes 8638976
  4855.7 36.1 all-reduce.13
  (676 shorter events, 1834.7 us)
Async XLA Ops:
  7.2 1206.2 %copy-start = (bf16[768,768]{1,0:T(8,128)(2,1)S(1)}, bf16[768,768]{1,0:T(8,128)(2,1)}, u32[]{:S(2)}) copy-start(bf16[768,768]{1,0:T(8,128)(2,1)} %param.36) | copy-start | bytes 3538948
  7.2 58.1 %all-gather.10.cloned.1.call-start = ((), (), s32[]{:S(2)}) async-start(), calls=%async_computation.4 | async-start | bytes 4362240 | tf_op jit(solution)/shard_map/all_gather | solution.py:158
  7.9 1200.8 %all-gather.14.cloned.1.call-start = ((), (), s32[]{:S(2)}) async-start(), calls=%async_computation.9 | async-start | bytes 4362240 | tf_op jit(solution)/shard_map/all_gather | solution.py:198
  8.0 57.0 %copy-start.49 = (f32[2,3,64]{2,0,1:T(2,128)S(1)}, f32[2,3,64]{2,0,1:T(2,128)}, u32[]{:S(2)}) copy-start(f32[2,3,64]{2,0,1:T(2,128)} %param.43) | copy-start | bytes 4612
  8.0 57.0 %copy-start.56 = (f32[2,192]{1,0:T(2,128)S(1)}, f32[2,192]{1,0:T(2,128)}, u32[]{:S(2)}) copy-start(f32[2,192]{1,0:T(2,128)} %param.31) | copy-start | bytes 4612
  8.0 57.2 %copy-start.30 = (f32[3,32]{1,0:T(4,128)S(1)}, f32[3,32]{1,0:T(4,128)}, u32[]{:S(2)}) copy-start(f32[3,32]{1,0:T(4,128)} %param.42) | copy-start | bytes 1156
  1090.4 66.9 %copy-start.57 = (u32[32]{0:T(128)S(1)}, u32[32]{0:T(128)}, u32[]{:S(2)}) copy-start(u32[32]{0:T(128)} %constant.234) | copy-start | bytes 388
  1090.4 76.6 %copy-start.6 = (bf16[1,561,768]{2,1,0:T(8,128)(2,1)S(1)}, bf16[1,561,768]{2,1,0:T(8,128)(2,1)}, u32[]{:S(2)}) copy-start(bf16[1,561,768]{2,1,0:T(8,128)(2,1)} %param.29) | copy-start | bytes 2585092
  1090.4 76.6 %copy-start.31 = (f32[768]{0:T(1024)S(1)}, f32[768]{0:T(1024)}, u32[]{:S(2)}) copy-start(f32[768]{0:T(1024)} %param.33) | copy-start | bytes 9220
  1155.1 21.0 copy-start.33
  1155.1 21.0 copy-start.35
  1156.0 6.8 collective-permute-start.2
  1158.6 8.9 collective-permute-start
  1177.7 147.5 %all-gather.16.cloned.1.call-start = ((), (), s32[]{:S(2)}) async-start(), calls=%async_computation.10 | async-start | bytes 4362240 | tf_op jit(solution)/shard_map/all_gather | solution.py:253
  1177.8 152.0 %copy-start.53 = (f32[768]{0:T(1024)}, f32[768]{0:T(1024)S(1)}, u32[]{:S(2)}) copy-start(f32[768]{0:T(1024)S(1)} %convert_element_type.299) | copy-start | bytes 9220
  1213.4 22.0 copy-start.58
  1239.6 44.0 copy-start.45
  1275.4 2.1 collective-permute-start.3
  1290.4 146.2 %all-gather.18.cloned.1.call-start = ((), (), s32[]{:S(2)}) async-start(), calls=%async_computation.11 | async-start | bytes 4362240 | tf_op jit(solution)/shard_map/all_gather | solution.py:268
  1383.7 2.1 collective-permute-start.4
  1399.3 41.8 copy-start.41
  1401.7 39.5 copy-start.22
  1401.7 3355.6 %all-gather.12.cloned.1.call-start = ((), (), s32[]{:S(2)}) async-start(), calls=%async_computation.8 | async-start | bytes 4362240 | tf_op jit(solution)/shard_map/all_gather | solution.py:198
  1402.3 3507.8 %reduce-scatter.25.cloned.1.call-start = ((), (), s32[]{:S(2)}) async-start(), calls=%async_computation.12 | async-start | bytes 884736
  1445.6 3466.1 %reduce-scatter.23.cloned.1.call-start = ((), (), s32[]{:S(2)}) async-start(), calls=%async_computation.7 | async-start | bytes 2654208 | tf_op jit(solution)/shard_map/reduce_scatter | solution.py:327
  1453.7 3458.0 %reduce-scatter.21.cloned.1.call-start = ((), (), s32[]{:S(2)}) async-start(), calls=%async_computation.6 | async-start | bytes 2654208 | tf_op jit(solution)/shard_map/reduce_scatter | solution.py:326
  1459.1 48.1 copy-start.29
  1466.6 3445.1 %reduce-scatter.19.cloned.1.call-start = ((), (), s32[]{:S(2)}) async-start(), calls=%async_computation.5 | async-start | bytes 2654208 | tf_op jit(solution)/shard_map/reduce_scatter | solution.py:324
  2268.9 14.6 copy-start.5
  2268.9 14.6 copy-start.3
  3072.2 14.6 copy-start.5
  3072.2 14.6 copy-start.3
  3875.3 14.6 copy-start.5
  3875.3 14.6 copy-start.3
  4678.5 14.6 copy-start.3
  4784.5 71.1 %copy-start.47 = (f32[4,2,3,64]{3,2,1,0:T(4,128)S(1)}, f32[4,2,3,64]{3,2,1,0:T(4,128)}, u32[]{:S(2)}) copy-start(f32[4,2,3,64]{3,2,1,0:T(4,128)} %get-tuple-element.467) | copy-start | bytes 18436
  4784.5 71.1 %copy-start.50 = (f32[4,3,32]{2,1,0:T(4,128)S(1)}, f32[4,3,32]{2,1,0:T(4,128)}, u32[]{:S(2)}) copy-start(f32[4,3,32]{2,1,0:T(4,128)} %get-tuple-element.466) | copy-start | bytes 4612
  4784.5 71.2 %copy-start.52 = (f32[768]{0:T(1024)S(1)}, f32[768]{0:T(1024)}, u32[]{:S(2)}) copy-start(f32[768]{0:T(1024)} %get-tuple-element.880) | copy-start | bytes 9220
  4784.5 119.9 %copy-start.7 = (bf16[1,561,768]{2,1,0:T(8,128)(2,1)S(1)}, bf16[1,561,768]{2,1,0:T(8,128)(2,1)}, u32[]{:S(2)}) copy-start(bf16[1,561,768]{2,1,0:T(8,128)(2,1)} %param.29) | copy-start | bytes 2585092
  4784.5 119.9 %copy-start.11 = (bf16[589,768]{1,0:T(8,128)(2,1)S(1)}, bf16[589,768]{1,0:T(8,128)(2,1)}, u32[]{:S(2)}) copy-start(bf16[589,768]{1,0:T(8,128)(2,1)} %concatenate.51) | copy-start | bytes 2714116
  4784.5 119.9 %copy-start.32 = (f32[768]{0:T(1024)S(1)}, f32[768]{0:T(1024)}, u32[]{:S(2)}) copy-start(f32[768]{0:T(1024)} %param.33) | copy-start | bytes 9220
  4784.6 119.9 %copy-start.34 = (f32[768]{0:T(1024)S(1)}, f32[768]{0:T(1024)}, u32[]{:S(2)}) copy-start(f32[768]{0:T(1024)} %param.34) | copy-start | bytes 9220
  4784.6 119.9 %copy-start.36 = (f32[768]{0:T(1024)S(1)}, f32[768]{0:T(1024)}, u32[]{:S(2)}) copy-start(f32[768]{0:T(1024)} %param.35) | copy-start | bytes 9220
  4784.6 119.9 %copy-start.38 = (f32[561]{0:T(1024)S(1)}, f32[561]{0:T(1024)}, u32[]{:S(2)}) copy-start(f32[561]{0:T(1024)} %copy-done.37) | copy-start | bytes 6736
  4784.6 119.9 %copy-start.40 = (f32[561]{0:T(1024)S(1)}, f32[561]{0:T(1024)}, u32[]{:S(2)}) copy-start(f32[561]{0:T(1024)} %copy-done.39) | copy-start | bytes 6736
  4784.6 119.9 %copy-start.46 = (f32[768]{0:T(1024)S(1)}, f32[768]{0:T(1024)}, u32[]{:S(2)}) copy-start(f32[768]{0:T(1024)} %param.39) | copy-start | bytes 9220
  4849.8 42.6 collective-permute-start.5
  4851.9 46.6 collective-permute-start.1
  (60 other events, 300.9 us)
Sparse Core Ops, SparseCore 0:
  9.6 33.1 all-gather.9
  1177.9 30.7 all-gather.13
  1290.5 34.6 all-gather.15
  1401.8 34.6 all-gather.17
  1438.5 30.4 all-gather.11
  1472.2 62.5 reduce-scatter.24
  1539.3 68.1 reduce-scatter.22
  1612.0 68.2 reduce-scatter.20
  4784.6 69.8 reduce-scatter.18
where the time goes:
time: 4950 us; the launch traced here: 4920 us
  local copies, waits for them, and re-layouts  3330 us (67%)
  matrix products  886 us (18%)
  blocking collectives  276 us (6%)
  other arithmetic  254 us (5%)
  waiting for transfers between devices  102 us (2%)
    eq x28, local copies, waits for them, and re-layouts, hot_mask(): bucket_ids[..., None] == jnp.arange(count, dtype=jnp.int32)  2320 us
    while x152, local copies, waits for them, and re-layouts  611 us
    dot_general x36, matrix products, table_bias(): jnp.einsum('qkb,hb->hqk', hot_mask(bucket_ids, count), both, preferred_el...  433 us
    slice x36, local copies, waits for them, and re-layouts, table_bias(): return summed[:heads_here] + summed[heads_here:]  230 us
    unnamed x4, blocking collectives  199 us
    dot_general x12, matrix products, table_grad(): jnp.einsum('hqk,qkb->hb', both, hot_mask(bucket_ids, count), preferred_el...  158 us
    eq x12, other arithmetic, hot_mask(): bucket_ids[..., None] == jnp.arange(count, dtype=jnp.int32)  154 us
    dot_general x12, matrix products, page_scores(): jnp.einsum('qhd,khd->hqk', page_q, page_k, preferred_element_type=jnp.flo...  127 us
  transfers between devices with their start and end apart: 15, of which 5 were waited for; matrix products, arithmetic and copies ran while one was open for 70% of the time, Pallas kernels for 0%

commit v1 on v0

v1 whole, which is shorter than its diff:
```python
import math

import jax
import jax.numpy as jnp
from jax import lax
from jax.experimental import pallas as pl
from jax.experimental.pallas import tpu as pltpu
from jax.sharding import PartitionSpec as P

f32 = jnp.float32
bf16 = jnp.bfloat16
i32 = jnp.int32
EPSILON = 1e-05
MASKED_SCORE = -1e30
HEAD_DIM=64; TEXT=512; NB1=32; MD1=128; NB2=64; MD2=256
ROWS=576
QROWS=640
LANES=128
VIS=ROWS-TEXT
BLOCKS=((0,256),(0,384),(128,384),(256,256),(0,576))
OFFS=[]; _t=0
for _i,(_s,_n) in enumerate(BLOCKS):
    OFFS.append(_t); _t+=_n+(VIS if _i<4 else 0)
TOTAL=_t

def thresholds(buckets, max_reach):
    half_range = buckets // 2
    exact_range = half_range // 2
    levels = half_range - exact_range
    return [math.ceil(exact_range * (max_reach / exact_range) ** (k / levels) - 1e-09) for k in range(1, levels)]

def bucket_of(diff, buckets, reach):
    n=jnp.abs(diff)
    out=jnp.minimum(n,buckets//4)+jnp.where(diff>0,buckets//2,0)
    for t in thresholds(buckets,reach):
        out=out+jnp.where(n>=t,1,0)
    return out

def windows():
    for i,(s,n) in enumerate(BLOCKS):
        yield i,s,n,OFFS[i]
        if i<4: yield i,TEXT,VIS,OFFS[i]+n

def ids_kernel(kcol_ref, qrow_ref, out_ref, *, rows_valid):
    for blk,s,n,o in windows():
        for c in range(0,n,64):
            seg=kcol_ref[s+c:s+c+64,0:1]; kx=kcol_ref[s+c:s+c+64,1:2]; ky=kcol_ref[s+c:s+c+64,2:3]
            ql=slice(blk*LANES,(blk+1)*LANES)
            qseg=qrow_ref[0:1,ql]; qx=qrow_ref[1:2,ql]; qy=qrow_ref[2:3,ql]
            kpos=lax.broadcasted_iota(i32,(64,LANES),0)+(s+c)
            qpos=lax.broadcasted_iota(i32,(64,LANES),1)+blk*LANES
            xid=bucket_of(jnp.broadcast_to(kx,(64,LANES))-qx,NB2,MD2)
            yid=bucket_of(jnp.broadcast_to(ky,(64,LANES))-qy,NB2,MD2)
            pid=bucket_of(kpos-qpos,NB1,MD1)
            ok=(jnp.broadcast_to(seg,(64,LANES))==qseg)|(kpos>=TEXT)|(qpos>=TEXT)
            ok=ok&(kpos<rows_valid)
            pid=jnp.where(ok,pid,NB1)
            out_ref[0,o+c:o+c+64,:]=xid
            out_ref[1,o+c:o+c+64,:]=yid+NB2
            out_ref[2,o+c:o+c+64,:]=pid

def make_ids(kcol,qrow,rows_valid):
    return pl.pallas_call(lambda a,b,c: ids_kernel(a,b,c,rows_valid=rows_valid),
        out_shape=jax.ShapeDtypeStruct((3,TOTAL,LANES),i32), name="ids",
        compiler_params=pltpu.CompilerParams(vmem_limit_bytes=32<<20))(kcol,qrow)

def nt(a,b): return lax.dot_general(a,b,(((1,),(1,)),((),())),preferred_element_type=f32)
def nn(a,b): return lax.dot_general(a,b,(((1,),(0,)),((),())),preferred_element_type=f32)
def take(tab,idx): return jnp.take_along_axis(jnp.broadcast_to(tab,idx.shape),idx,axis=1,mode="promise_in_bounds")

def head_cols(h):
    j,l=divmod(h,3)
    return [j*576+p*192+l*64 for p in range(3)]

def fwd_kernel(mixed_ref, ids_ref, tab_ref, out_ref, p_ref, q_s, k_s, vt_s, s_s, o_s, *, heads):
    for h in range(heads):
        cq,ck,cv=head_cols(h)
        q_s[h,0:ROWS,:]=mixed_ref[:,cq:cq+64]
        q_s[h,ROWS:QROWS,:]=jnp.zeros((QROWS-ROWS,64),bf16)
        k_s[h]=mixed_ref[:,ck:ck+64]
        vt_s[h]=mixed_ref[:,cv:cv+64].astype(f32).T.astype(bf16)
    def head(h,_):
        txy=tab_ref[pl.ds(2*h,1),:]; tp=tab_ref[pl.ds(2*h+1,1),:]
        for blk in range(5):
            q=q_s[h,blk*LANES:(blk+1)*LANES,:]
            parts=[(s,n,o) for b,s,n,o in windows() if b==blk]
            m=jnp.full((1,LANES),-3e38,f32)
            for s,n,o in parts:
                sc=nt(k_s[h,s:s+n,:],q)
                for c in range(0,n,64):
                    r=slice(o+c,o+c+64)
                    v=sc[c:c+64]+(take(tp,ids_ref[2,r,:])+(take(txy,ids_ref[0,r,:])+take(txy,ids_ref[1,r,:])))
                    s_s[o-OFFS[blk]+c:o-OFFS[blk]+c+64,:]=v
                    m=jnp.maximum(m,jnp.max(v,axis=0,keepdims=True))
            l=jnp.zeros((1,LANES),f32)
            tot=sum(n for _,n,_ in parts)
            for c in range(0,tot,64):
                e=jnp.exp(s_s[c:c+64,:]-m)
                s_s[c:c+64,:]=e
                l=l+jnp.sum(e,axis=0,keepdims=True)
            inv=1.0/l
            for c in range(0,tot,64):
                p_ref[h,OFFS[blk]+c:OFFS[blk]+c+64,:]=(s_s[c:c+64,:]*inv).astype(bf16)
            ot=jnp.zeros((64,LANES),f32)
            for s,n,o in parts:
                ot=ot+nn(vt_s[h,:,s:s+n],p_ref[h,o:o+n,:])
            o_s[h,blk*LANES:(blk+1)*LANES,:]=ot.T
        return 0
    lax.fori_loop(0,heads,head,0)
    for h in range(heads):
        out_ref[:,h*64:h*64+64]=o_s[h,0:ROWS,:].astype(bf16)

def attn_fwd(mixed,ids,tab,heads=12):
    return pl.pallas_call(lambda *a: fwd_kernel(*a,heads=heads),
        out_shape=(jax.ShapeDtypeStruct((ROWS,heads*64),bf16),jax.ShapeDtypeStruct((heads,TOTAL,LANES),bf16)),
        scratch_shapes=[pltpu.VMEM((heads,QROWS,64),bf16),pltpu.VMEM((heads,ROWS,64),bf16),pltpu.VMEM((heads,64,ROWS),bf16),
            pltpu.VMEM((ROWS,LANES),f32),pltpu.VMEM((heads,QROWS,64),f32)], name="attn_fwd",
        compiler_params=pltpu.CompilerParams(vmem_limit_bytes=56<<20))(mixed,ids,tab)

STEP=16
def bwd_kernel(mixed_ref, do_ref, p_ref, ids_ref, out_ref, hist_ref, q_s, k_s, kt_s, v_s, do_s, dq_s, dk_s, dv_s, ds_s, *, heads):
    for h in range(heads):
        cq,ck,cv=head_cols(h)
        q_s[h,0:ROWS,:]=mixed_ref[:,cq:cq+64]
        q_s[h,ROWS:QROWS,:]=jnp.zeros((QROWS-ROWS,64),bf16)
        do_s[h,0:ROWS,:]=do_ref[:,h*64:h*64+64]
        do_s[h,ROWS:QROWS,:]=jnp.zeros((QROWS-ROWS,64),bf16)
        kk=mixed_ref[:,ck:ck+64]
        k_s[h]=kk
        kt_s[h]=kk.astype(f32).T.astype(bf16)
        v_s[h]=mixed_ref[:,cv:cv+64]
    for h in range(heads,16):
        ds_s[pl.ds(h,TOTAL,stride=16),:]=jnp.zeros((TOTAL,LANES),f32)
    def head(h,_):
        for blk in range(5):
            q=q_s[h,blk*LANES:(blk+1)*LANES,:]; do=do_s[h,blk*LANES:(blk+1)*LANES,:]
            parts=[(s,n,o) for b,s,n,o in windows() if b==blk]
            dps=[nt(v_s[h,s:s+n,:],do) for s,n,o in parts]
            D=jnp.zeros((1,LANES),f32)
            for (s,n,o),dp in zip(parts,dps):
                for c in range(0,n,64):
                    D=D+jnp.sum(p_ref[h,o+c:o+c+64,:].astype(f32)*dp[c:c+64],axis=0,keepdims=True)
            dqt=jnp.zeros((64,LANES),f32)
            for (s,n,o),dp in zip(parts,dps):
                dsb=[]
                for c in range(0,n,64):
                    ds=p_ref[h,o+c:o+c+64,:].astype(f32)*(dp[c:c+64]-D)
                    ds_s[pl.ds((o+c)*16+h,64,stride=16),:]=ds
                    dsb.append(ds.astype(bf16))
                dsb=jnp.concatenate(dsb,0)
                dqt=dqt+nn(kt_s[h,:,s:s+n],dsb)
                dv=nn(p_ref[h,o:o+n,:],do); dk=nn(dsb,q)
                if blk==0:
                    dv_s[h,s:s+n,:]=dv; dk_s[h,s:s+n,:]=dk
                elif blk==1 and s==0:
                    dv_s[h,0:256,:]+=dv[0:256]; dk_s[h,0:256,:]+=dk[0:256]
                    dv_s[h,256:384,:]=dv[256:]; dk_s[h,256:384,:]=dk[256:]
                elif blk==2 and s==128:
                    dv_s[h,128:384,:]+=dv[0:256]; dk_s[h,128:384,:]+=dk[0:256]
                    dv_s[h,384:512,:]=dv[256:]; dk_s[h,384:512,:]=dk[256:]
                else:
                    dv_s[h,s:s+n,:]+=dv; dk_s[h,s:s+n,:]+=dk
            dq_s[h,blk*LANES:(blk+1)*LANES,:]=dqt.T*0.125
        return 0
    lax.fori_loop(0,heads,head,0)
    for h in range(heads):
        cq,ck,cv=head_cols(h)
        out_ref[:,cq:cq+64]=dq_s[h,0:ROWS,:].astype(bf16)
        out_ref[:,ck:ck+64]=dk_s[h].astype(bf16)
        out_ref[:,cv:cv+64]=dv_s[h].astype(bf16)
    io=lax.broadcasted_iota(i32,(64,LANES),0)
    io2=io+64
    def rows(r,acc):
        lhs=[];rhs=[]
        for u in range(STEP):
            k=r*STEP+u
            x=ids_ref[0,pl.ds(k,1),:]; y=ids_ref[1,pl.ds(k,1),:]; p=ids_ref[2,pl.ds(k,1),:]
            rhs.append(jnp.concatenate([jnp.where(io==x,1.,0.),jnp.where(io2==y,1.,0.),jnp.where(io[:32]==p,1.,0.)],0).astype(bf16))
            lhs.append(ds_s[pl.ds(pl.multiple_of(k*16,16),16),:].astype(bf16))
        return acc+nt(jnp.concatenate(lhs,1),jnp.concatenate(rhs,1))
    hist_ref[...]=lax.fori_loop(0,TOTAL//STEP,rows,jnp.zeros((16,160),f32))

def attn_bwd(mixed,d_att,p,ids,heads=12):
    return pl.pallas_call(lambda *a: bwd_kernel(*a,heads=heads),
        out_shape=(jax.ShapeDtypeStruct((ROWS,heads*192),bf16),jax.ShapeDtypeStruct((16,160),f32)),
        scratch_shapes=[pltpu.VMEM((heads,QROWS,64),bf16),pltpu.VMEM((heads,ROWS,64),bf16),pltpu.VMEM((heads,64,ROWS),bf16),
            pltpu.VMEM((heads,ROWS,64),bf16),pltpu.VMEM((heads,QROWS,64),bf16),
            pltpu.VMEM((heads,QROWS,64),f32),pltpu.VMEM((heads,ROWS,64),f32),pltpu.VMEM((heads,ROWS,64),f32),
            pltpu.VMEM((TOTAL*16,LANES),f32)], name="attn_bwd",
        compiler_params=pltpu.CompilerParams(vmem_limit_bytes=60<<20))(mixed,d_att,p,ids)


def core_swap(v):
    return lax.ppermute(v, "heads", [(i, i ^ 1) for i in range(4)])


def x_swap(v):
    return lax.ppermute(v, "heads", [(i, i ^ 2) for i in range(4)])


def collect(shard):
    pair = jnp.concatenate((shard, x_swap(shard)), axis=0)
    return jnp.concatenate((pair, core_swap(pair)), axis=0)


def reduce_pages(part):
    pages = lax.axis_size("pages")
    me = lax.axis_index("pages")
    rows, cols = part.shape
    cur = part.reshape(pages, rows // pages, cols)
    bit = 1
    while bit < pages:
        view = cur.reshape(-1, 2, rows // pages, cols)
        mine = (me // bit) % 2
        keep = lax.dynamic_index_in_dim(view, mine, axis=1, keepdims=False)
        send = lax.dynamic_index_in_dim(view, 1 - mine, axis=1, keepdims=False)
        got = lax.ppermute(send, "pages", [(i, i ^ bit) for i in range(pages)])
        cur = keep.astype(f32) + got.astype(f32)
        bit *= 2
        if bit < pages:
            cur = cur.astype(bf16)
    return cur.reshape(rows // pages, cols)


def tn(a, b):
    return lax.dot_general(a, b, (((0,), (0,)), ((), ())), preferred_element_type=f32)


def reduce_heads(rows_mat, col_mat):
    width = col_mat.shape[1] // 4
    send = tn(rows_mat, col_mat[:, 2 * width :]).astype(bf16)
    got = core_swap(send)
    far = (tn(rows_mat, col_mat[:, width : 2 * width]) + got[:, width:].astype(f32)).astype(bf16)
    got_far = x_swap(far)
    own = tn(rows_mat, col_mat[:, :width]) + got[:, :width].astype(f32) + got_far.astype(f32)
    return own.astype(bf16)


def norm_parts(values):
    centered = values - jnp.mean(values, axis=-1, keepdims=True)
    inv_std = lax.rsqrt(jnp.mean(centered * centered, axis=-1, keepdims=True) + EPSILON)
    return centered * inv_std, inv_std


def norm_back(unit, inv_std, gain, dy):
    e = dy * gain
    dv = inv_std * (
        e - jnp.mean(e, axis=-1, keepdims=True) - unit * jnp.mean(e * unit, axis=-1, keepdims=True)
    )
    return dv, jnp.sum(dy * unit, axis=0), jnp.sum(dy, axis=0)


def on_device(
    tokens,
    w_qkv,
    qv_bias,
    w_out,
    out_bias,
    norm1_gain,
    norm1_shift,
    w_up,
    up_bias,
    w_down,
    down_bias,
    norm2_gain,
    norm2_shift,
    pos_table,
    box_table,
    receipt_lengths,
    page_boxes,
    out_cotangent,
):
    seq_len = tokens.shape[1]
    width = tokens.shape[2]
    heads_here = pos_table.shape[0]
    inner = heads_here * HEAD_DIM
    heads_all = 4 * heads_here
    units = w_up.shape[1]
    spare = ROWS - seq_len
    own_page = lax.axis_index("heads")

    wt_qkv = collect(w_qkv.reshape(width, 3 * inner).T)
    table_row = jnp.zeros((heads_here, 2, LANES), f32)
    table_row = table_row.at[:, 0, :NB2].set(box_table[0]).at[:, 0, NB2:].set(box_table[1])
    table_row = table_row.at[:, 1, :NB1].set(pos_table).at[:, 1, NB1].set(MASKED_SCORE)
    small = jnp.concatenate(
        (table_row.reshape(-1), qv_bias.reshape(-1), up_bias.astype(f32))
    )
    small = collect(small.reshape(1, -1))
    n_tab = heads_here * 2 * LANES
    tables = small[:, :n_tab].reshape(heads_all * 2, LANES)
    qv_all = small[:, n_tab : n_tab + 2 * inner].reshape(4, 2, inner)
    up_bias_all = small[:, n_tab + 2 * inner :].reshape(4 * units)
    wt_out = collect(w_out)
    wt_up = collect(w_up.T)
    wt_down = collect(w_down)

    lengths = lax.dynamic_index_in_dim(receipt_lengths, own_page, 0, keepdims=False)
    boxes = lax.dynamic_index_in_dim(page_boxes, own_page, 0, keepdims=False)
    ends = jnp.cumsum(lengths, dtype=i32)
    segment = jnp.sum((jnp.arange(QROWS, dtype=i32)[None, :] >= ends[:, None]).astype(i32), axis=0)
    q_row = jnp.concatenate((segment[None], jnp.pad(boxes, ((0, 0), (0, QROWS - seq_len)))), axis=0)
    k_col = jnp.pad(q_row[:, :ROWS].T, ((0, 0), (0, LANES - 3)))
    q_row = jnp.pad(q_row, ((0, 5), (0, 0)))
    ids = make_ids(k_col, q_row, seq_len)

    tok = jnp.pad(tokens.reshape(seq_len, width), ((0, spare), (0, 0)))
    ct = jnp.pad(out_cotangent.reshape(seq_len, width), ((0, spare), (0, 0))).astype(f32)
    tok32 = tok.astype(f32)

    bias_row = jnp.concatenate(
        (qv_all[:, 0:1], jnp.zeros((4, 1, inner), f32), qv_all[:, 1:2]), axis=1
    ).reshape(1, -1)
    scale_row = jnp.concatenate(
        (jnp.full((4, 1, inner), 0.125, f32), jnp.ones((4, 2, inner), f32)), axis=1
    ).reshape(1, -1)
    mixed = ((nt(tok, wt_qkv) + bias_row) * scale_row).astype(bf16)
    attended, probs = attn_fwd(mixed, ids, tables, heads_all)
    first_in = nn(attended, wt_out) + out_bias + tok32
    unit1, inv1 = norm_parts(first_in)
    first_out = unit1 * norm1_gain + norm1_shift
    first_low = first_out.astype(bf16)
    up = nt(first_low, wt_up) + up_bias_all
    cdf = 0.5 * (1.0 + lax.erf(up * math.sqrt(0.5)))
    hidden = (up * cdf).astype(bf16)
    slope = (cdf + up * jnp.exp(-0.5 * up * up) * (1.0 / math.sqrt(2.0 * math.pi))).astype(bf16)
    second_in = nn(hidden, wt_down) + down_bias + first_out
    unit2, inv2 = norm_parts(second_in)
    layer_out = (unit2 * norm2_gain + norm2_shift).astype(bf16)

    d_second, g_gain2, g_shift2 = norm_back(unit2, inv2, norm2_gain, ct)
    g_down_bias = jnp.sum(d_second, axis=0)
    d_ffn = d_second.astype(bf16)
    r_down = reduce_heads(d_ffn, hidden)
    d_up = (nt(d_ffn, wt_down) * slope.astype(f32)).astype(bf16)
    r_up = reduce_heads(first_low, d_up)
    g_up_bias = jnp.sum(d_up.astype(f32), axis=0)
    d_mid = nn(d_up, wt_up)
    d_first, g_gain1, g_shift1 = norm_back(unit1, inv1, norm1_gain, d_second + d_mid)
    g_out_bias = jnp.sum(d_first, axis=0)
    d_proj = d_first.astype(bf16)
    r_out = reduce_heads(d_proj, attended)
    d_attended = nt(d_proj, wt_out).astype(bf16)
    d_mixed, hist = attn_bwd(mixed, d_attended, probs, ids, heads_all)
    r_qkv = reduce_heads(tok, d_mixed)
    grad_tokens = (nn(d_mixed, wt_qkv) + d_first)[:seq_len].astype(bf16)

    g_w_down = reduce_pages(r_down).T
    g_w_up = reduce_pages(r_up)
    g_w_out = reduce_pages(r_out).T
    g_w_qkv = reduce_pages(r_qkv).reshape(-1, 3, inner)

    mixed_sums = jnp.sum(d_mixed.astype(f32), axis=0).reshape(4, 3, inner)
    split = jnp.concatenate(
        (
            mixed_sums[:, 0],
            mixed_sums[:, 2],
            hist[:heads_all].reshape(4, heads_here * 160),
            g_up_bias.reshape(4, units),
        ),
        axis=1,
    )
    split = split[:2] + core_swap(split[2:])
    split = split[0] + x_swap(split[1])
    split = lax.psum(split, "pages")
    g_qv_bias = split[: 2 * inner].reshape(2, inner)
    tab = split[2 * inner : 2 * inner + heads_here * 160].reshape(heads_here, 160)
    g_up_bias = split[2 * inner + heads_here * 160 :]
    g_box = jnp.stack((tab[:, :NB2], tab[:, NB2 : 2 * NB2]))
    g_pos = tab[:, 2 * NB2 :]
    shared = lax.psum(
        jnp.stack((g_out_bias, g_gain1, g_shift1, g_down_bias, g_gain2, g_shift2)),
        ("pages", "heads"),
    )
    return (
        layer_out[:seq_len].reshape(tokens.shape),
        grad_tokens.reshape(tokens.shape),
        g_w_qkv,
        g_qv_bias,
        g_w_out,
        shared[0],
        shared[1],
        shared[2],
        g_w_up,
        g_up_bias,
        g_w_down,
        shared[3],
        shared[4],
        shared[5],
        g_pos,
        g_box,
    )


def solution(mesh):
    placed = (
        P(("pages", "heads"), None, None),
        P(None, None, "heads"),
        P(None, "heads"),
        P("heads", None),
        P(),
        P(),
        P(),
        P(None, "heads"),
        P("heads"),
        P("heads", None),
        P(),
        P(),
        P(),
        P("heads", None),
        P(None, "heads", None),
        P("pages", None),
        P("pages", None, None),
        P(("pages", "heads"), None, None),
    )
    return jax.shard_map(
        on_device,
        mesh=mesh,
        in_specs=placed,
        out_specs=(
            P(("pages", "heads"), None, None),
            P(("pages", "heads"), None, None),
            P("pages", None, "heads"),
            P(None, "heads"),
            P("heads", "pages"),
            P(),
            P(),
            P(),
            P("pages", "heads"),
            P("heads"),
            P("heads", "pages"),
            P(),
            P(),
            P(),
            P("heads", None),
            P(None, "heads", None),
        ),
        check_vma=False,
    )
```

time: 4950 us -> 484 us (0.10)
  local copies, waits for them, and re-layouts: 3330 us -> 34.6 us
  matrix products: 886 us -> 73.7 us
  other arithmetic: 254 us -> 34.6 us
  blocking collectives: 276 us -> 61.1 us
  Pallas kernels: 0 us -> 120 us
    eq x28 -> x0, local copies, waits for them, and re-layouts: 2320 us -> none  [hot_mask(): bucket_ids[..., None] == jnp.arange(count, dtype=jnp.int32)]
    dot_general x97 -> x20, matrix products: 882 us -> 73.7 us  [the longest x12 35.9 us: tn(): lax.dot_general(a, b, (((0,), (0,)), ((), ())), preferred_element_type=f32)]
    while x156 -> x0, local copies, waits for them, and re-layouts: 618 us -> none
    slice x44 -> x9, local copies, waits for them, and re-layouts: 233 us -> 1.96 us  [the longest x1 0.66 us: on_device(): g_up_bias = split[2 * inner + heads_here * 160:]]
    unnamed x4 -> x0, blocking collectives: 199 us -> none
    eq x12 -> x0, other arithmetic: 154 us -> none  [hot_mask(): bucket_ids[..., None] == jnp.arange(count, dtype=jnp.int32)]
    ppermute x0 -> x32, waiting for transfers between devices: none -> 131 us  [the longest x10 99.4 us: x_swap(): return lax.ppermute(v, 'heads', [(i, i ^ 2) for i in range(4)])]
    pallas_call x0 -> x3, Pallas kernels: none -> 120 us  [the longest x1 76 us: attn_bwd(): pl.pallas_call(lambda *a: bwd_kernel(*a, heads=heads), out_shape=(jax.Sha...]
  transfers between devices with their start and end apart: 15 -> 32, of which waited for: 5 -> 12; matrix products, arithmetic and copies ran while one was open for 70% -> 15% of each run, Pallas kernels for 0% -> 9%
where the time goes in v1:
time: 484 us; the launch traced here: 475 us
  waiting for transfers between devices  131 us (27%)
  Pallas kernels  120 us (25%)
  matrix products  73.7 us (15%)
  blocking collectives  61.1 us (13%)
  local copies, waits for them, and re-layouts  34.6 us (7%)
  other arithmetic  34.6 us (7%)
  starting transfers between devices  18.1 us (4%)
    ppermute x10, waiting for transfers between devices, x_swap(): return lax.ppermute(v, 'heads', [(i, i ^ 2) for i in range(4)])  99.4 us
    pallas_call x1, Pallas kernels, attn_bwd(): pl.pallas_call(lambda *a: bwd_kernel(*a, heads=heads), out_shape=(jax.Sha...  76 us
    psum x1, blocking collectives, on_device(): lax.psum(jnp.stack((g_out_bias, g_gain1, g_shift1, g_down_bias, g_gain2,...  40.1 us
    pallas_call x1, Pallas kernels, attn_fwd(): pl.pallas_call(lambda *a: fwd_kernel(*a, heads=heads), out_shape=(jax.Sha...  39.8 us
    dot_general x12, matrix products, tn(): lax.dot_general(a, b, (((0,), (0,)), ((), ())), preferred_element_type=f32)  35.9 us
    ppermute x12, waiting for transfers between devices, reduce_pages(): got = lax.ppermute(send, 'pages', [(i, i ^ bit) for i in range(pages)])  31.3 us
    psum x1, blocking collectives, on_device(): split = lax.psum(split, 'pages')  21 us
    dot_general x4, matrix products, nt(): lax.dot_general(a, b, (((1,), (1,)), ((), ())), preferred_element_type=f32)  20.4 us
  transfers between devices with their start and end apart: 32, of which 12 were waited for; matrix products, arithmetic and copies ran while one was open for 15% of the time, Pallas kernels for 9%

profile of v1, /device:TPU:0, one launch (start us, length us, event | category | flops | bytes accessed | tf_op | source)
XLA Modules:
  0.0 475.0 jit_solution(5146143946082388018)
XLA Ops:
  4.0 2.7 broadcast_select_fusion
  6.7 1.9 scatter.15
  10.5 3.0 collective-permute-start.2
  13.6 1.9 collective-permute-start
  15.7 1.9 collective-permute-start.8
  20.3 2.3 constant_dynamic-update-slice_fusion.5
  23.1 4.4 ids.1.a_1_.a_3_
  27.6 15.1 %collective-permute-done = bf16[576,768]{1,0:T(8,128)(2,1)} collective-permute-done((bf16[576,768]{1,0:T(8,128)(2,1)}, bf16[576,768]{1,0:T(8,128)(2,1)}, u32[]{:S(2)}, u32[]{:S(2)}) %collective-permute-start) | collective-permute-done | bytes 884768 | tf_op jit(solution)/shard_map/ppermute | solution.py:198
  42.8 2.5 pad_maximum_fusion.6
  48.2 43.6 %collective-permute-done.8 = bf16[768,768]{1,0:T(8,128)(2,1)S(1)} collective-permute-done((bf16[768,768]{1,0:T(8,128)(2,1)}, bf16[768,768]{1,0:T(8,128)(2,1)S(1)}, u32[]{:S(2)}, u32[]{:S(2)}) %collective-permute-start.8) | collective-permute-done | bytes 1179680 | tf_op jit(solution)/shard_map/ppermute | solution.py:198
  92.0 3.0 pad_maximum_fusion.2
  96.9 5.5 %multiply_convert_fusion.2.a_0_ = bf16[576,2304]{1,0:T(8,128)(2,1)} fusion(f32[2304]{0:T(1024)S(1)} %copy-done.44, f32[2304]{0:T(1024)S(1)} %add.267, bf16[1152,768]{1,0:T(8,128)(2,1)} %collective-permute-done.1, bf16[576,768]{1,0:T(8,128)(2,1)} %collective-permute-done, bf16[576,768]{1,0:T(8,128)(2,1)S(1)} %bitcast.144, bf16[561,768]{1,0:T(8,128)(2,1)S(1)} %bitcast.147), kind=kOutput, calls=%fused_computation.11 | convolution fusion | flops 2053029888 | bytes 7073280 | tf_op jit(solution)/shard_map/dot_general | solution.py:67
  102.5 39.8 %attn_fwd.1 = (bf16[576,768]{1,0:T(8,128)(2,1)}, bf16[12,2112,128]{2,1,0:T(8,128)(2,1)}) custom-call(bf16[576,2304]{1,0:T(8,128)(2,1)} %multiply_convert_fusion.2.a_0_, s32[3,2112,128]{2,1,0:T(8,128)} %copy-done.2, f32[24,128]{1,0:T(8,128)} %reshape.371.a_2_), custom_call_target="tpu_custom_call" | custom-call | tf_op jit(solution)/shard_map/attn_fwd/pallas_call | solution.py:114
  142.3 2.1 fusion.80
  145.5 1.7 constant_dynamic-update-slice_fusion.3
  147.2 6.5 %multiply_convert_fusion.1 = (bf16[576,3072]{1,0:T(8,128)(2,1)S(1)}, f32[576,3072]{1,0:T(8,128)S(1)}) fusion(f32[3072]{0:T(1024)S(1)} %copy-done.39, bf16[576,768]{1,0:T(8,128)(2,1)S(1)} %fusion.19, bf16[1536,768]{0,1:T(8,128)(2,1)} %collective-permute-done.7, bf16[768,768]{0,1:T(8,128)(2,1)} %collective-permute-done.6, bf16[768,768]{0,1:T(8,128)(2,1)S(1)} %bitcast.140), kind=kOutput, calls=%fused_computation.8 | convolution fusion | flops 2742681600 | bytes 16232448 | tf_op jit(solution)/shard_map/dot_general | solution.py:67
  153.7 3.1 fusion.81
  160.6 6.7 %convert_reduce_fusion = (f32[3072]{0:T(1024)}, bf16[576,3072]{1,0:T(8,128)(2,1)S(1)}) fusion(f32[576,3072]{1,0:T(8,128)S(1)} %get-tuple-element.140, f32[3072]{0:T(1024)S(1)} %copy-done.39, bf16[576,768]{1,0:T(8,128)(2,1)S(1)} %convert_element_type.260, bf16[3072,768]{1,0:T(8,128)(2,1)S(1)} %copy-done.29), kind=kOutput, calls=%fused_computation.6 | convolution fusion | flops 2744448000 | bytes 16244736 | tf_op jit(solution)/shard_map/dot_general | solution.py:67
  167.3 8.2 %multiply_reduce_fusion = (f32[768]{0:T(1024)}, f32[576]{0:T(1024)S(1)}, f32[576]{0:T(1024)S(1)}, f32[768]{0:T(1024)}, f32[576,768]{1,0:T(8,128)S(1)}) fusion(f32[576,768]{1,0:T(8,128)S(1)} %get-tuple-element.138, f32[576]{0:T(1024)S(1)} %add_rsqrt_fusion.1, f32[576]{0:T(1024)S(1)} %broadcast_multiply_fusion.5, f32[768]{0:T(1024)S(1)} %copy-done.38, ...), kind=kOutput, calls=%fused_computation.38 | convolution fusion | flops 2736485888 | bytes 13584384 | tf_op jit(solution)/shard_map/dot_general | solution.py:68
  177.9 1.8 convolution_convert_fusion.3.a_1_
  181.7 76.0 %attn_bwd.1 = (bf16[576,2304]{1,0:T(8,128)(2,1)}, f32[16,160]{1,0:T(8,128)}) custom-call(bf16[576,2304]{1,0:T(8,128)(2,1)} %multiply_convert_fusion.2.a_0_, bf16[576,768]{1,0:T(8,128)(2,1)} %convolution_convert_fusion.3.a_1_, bf16[12,2112,128]{2,1,0:T(8,128)(2,1)} %get-tuple-element.69.a_2_, s32[3,2112,128]{2,1,0:T(8,128)} %copy-done.2), custom_call_target="tpu_custom_call" | custom-call | tf_op jit(solution)/shard_map/attn_bwd/pallas_call | solution.py:184
  257.7 3.0 convert_reduce_fusion.1
  260.7 4.1 convolution_convert_fusion.2
  264.8 2.2 fusion.44
  267.0 3.8 fusion.36
  270.8 3.5 convolution_convert_fusion
  274.3 2.5 fusion.30
  278.2 3.9 fusion.21
  290.7 40.1 %psum.15 = f32[6,768]{1,0:T(8,128)S(1)} all-reduce(f32[6,768]{1,0:T(8,128)S(1)} %stack.36), channel_id=1, replica_groups=mesh['pages'=8,'heads'=4] {'pages','heads'}, use_global_device_ids=true, to_apply=%region_20.21 | all-reduce | flops 4608 | bytes 36864 | tf_op jit(solution)/shard_map/psum | solution.py:371
  330.8 5.1 %convolution_convert_fusion.1 = bf16[768,1536]{1,0:T(8,128)(2,1)} fusion(bf16[576,768]{1,0:T(8,128)(2,1)S(1)} %copy-done.18, bf16[576,3072]{1,0:T(8,128)(2,1)} %copy-done.47), kind=kOutput, calls=%fused_computation.15 | convolution fusion | flops 1360134144 | bytes 5013504 | tf_op jit(solution)/shard_map/dot_general | solution.py:226
  337.6 2.3 collective-permute-start.18
  340.7 5.5 %collective-permute-done.16 = f32[1632]{0:T(1024)S(1)} collective-permute-done((f32[1632]{0:T(1024)S(1)}, f32[1632]{0:T(1024)S(1)}, u32[]{:S(2)}, u32[]{:S(2)}) %collective-permute-start.16) | collective-permute-done | bytes 6560 | tf_op jit(solution)/shard_map/ppermute | solution.py:198
  346.2 21.0 %psum.14 = f32[1632]{0:T(1024)S(1)} all-reduce(f32[1632]{0:T(1024)S(1)} %add.307), channel_id=1, replica_groups=mesh['pages'=8,'heads'=4] {'pages'}, use_global_device_ids=true, to_apply=%region_13.14 | all-reduce | flops 1632 | bytes 13056 | tf_op jit(solution)/shard_map/psum | solution.py:365
  369.2 3.7 add_convert_fusion.5
  377.5 3.4 collective-permute-done.20
  381.5 7.3 %collective-permute-done.11 = bf16[768,576]{0,1:T(8,128)(2,1)S(1)} collective-permute-done((bf16[768,576]{0,1:T(8,128)(2,1)}, bf16[768,576]{0,1:T(8,128)(2,1)S(1)}, u32[]{:S(2)}, u32[]{:S(2)}) %collective-permute-start.11) | collective-permute-done | bytes 884768 | tf_op jit(solution)/shard_map/ppermute | solution.py:198
  391.0 1.8 collective-permute-start.12
  392.8 3.7 add_convert_fusion.1
  396.7 3.7 add_convert_fusion.3
  400.5 1.7 collective-permute-start.23
  405.8 5.3 %collective-permute-done.13 = bf16[2,96,576]{2,1,0:T(8,128)(2,1)S(1)} collective-permute-done((bf16[2,96,576]{2,1,0:T(8,128)(2,1)S(1)}, bf16[2,96,576]{2,1,0:T(8,128)(2,1)S(1)}, u32[]{:S(2)}, u32[]{:S(2)}) %collective-permute-start.13) | collective-permute-done | bytes 221216 | tf_op jit(solution)/shard_map/ppermute | solution.py:217
  412.2 13.5 %collective-permute-done.28 = bf16[768,768]{1,0:T(8,128)(2,1)} collective-permute-done((bf16[768,768]{1,0:T(8,128)(2,1)}, bf16[768,768]{1,0:T(8,128)(2,1)}, u32[]{:S(2)}, u32[]{:S(2)}) %collective-permute-start.28) | collective-permute-done | bytes 1179680 | tf_op jit(solution)/shard_map/ppermute | solution.py:198
  425.7 2.1 add_convert_fusion
  428.3 14.4 %collective-permute-done.23 = bf16[768,768]{1,0:T(8,128)(2,1)} collective-permute-done((bf16[768,768]{1,0:T(8,128)(2,1)}, bf16[768,768]{1,0:T(8,128)(2,1)}, u32[]{:S(2)}, u32[]{:S(2)}) %collective-permute-start.23) | collective-permute-done | bytes 1179680 | tf_op jit(solution)/shard_map/ppermute | solution.py:198
  442.7 2.1 add_convert_fusion.2
  448.7 7.2 %collective-permute-done.24 = bf16[4,96,768]{2,1,0:T(8,128)(2,1)} collective-permute-done((bf16[4,96,768]{2,1,0:T(8,128)(2,1)}, bf16[4,96,768]{2,1,0:T(8,128)(2,1)}, u32[]{:S(2)}, u32[]{:S(2)}) %collective-permute-start.24) | collective-permute-done | bytes 589856 | tf_op jit(solution)/shard_map/ppermute | solution.py:217
  458.5 8.5 %collective-permute-done.25 = bf16[2,96,768]{2,1,0:T(8,128)(2,1)S(1)} collective-permute-done((bf16[2,96,768]{2,1,0:T(8,128)(2,1)S(1)}, bf16[2,96,768]{2,1,0:T(8,128)(2,1)S(1)}, u32[]{:S(2)}, u32[]{:S(2)}) %collective-permute-start.25) | collective-permute-done | bytes 294944 | tf_op jit(solution)/shard_map/ppermute | solution.py:217
  468.0 5.9 %collective-permute-done.26 = bf16[1,96,768]{2,1,0:T(8,128)(2,1)S(1)} collective-permute-done((bf16[1,96,768]{2,1,0:T(8,128)(2,1)S(1)}, bf16[1,96,768]{2,1,0:T(8,128)(2,1)S(1)}, u32[]{:S(2)}, u32[]{:S(2)}) %collective-permute-start.26) | collective-permute-done | bytes 147488 | tf_op jit(solution)/shard_map/ppermute | solution.py:217
  (264 shorter events, 58.0 us)
Async XLA Ops:
  0.6 17.9 %copy-start = (s32[4,2,561]{2,1,0:T(2,128)S(1)}, s32[4,2,561]{2,1,0:T(2,128)}, u32[]{:S(2)}) copy-start(s32[4,2,561]{2,1,0:T(2,128)} %param.42) | copy-start | bytes 53860
  10.5 17.0 %collective-permute-start.2 = (f32[1,1920]{1,0:T(1,128)S(1)}, f32[1,1920]{1,0:T(1,128)S(1)}, u32[]{:S(2)}, u32[]{:S(2)}) collective-permute-start(f32[1,1920]{1,0:T(1,128)S(1)} %reshape.367), channel_id=1, source_target_pairs={{0,2},{1,3},{2,0},{3,1},{4,6},{5,7},{6,4},{7,5},{8,10},{9,11},{10,... | collective-permute-start | bytes 23048 | tf_op jit(solution)/shard_map/ppermute | solution.py:198
  13.5 33.3 %collective-permute-start.4 = (bf16[192,768]{1,0:T(8,128)(2,1)}, bf16[192,768]{1,0:T(8,128)(2,1)S(1)}, u32[]{:S(2)}, u32[]{:S(2)}) collective-permute-start(bf16[192,768]{1,0:T(8,128)(2,1)} %param.29), channel_id=1, source_target_pairs={{0,2},{1,3},{2,0},{3,1},{4,6},{5,7},{6,4},{7,5},{8,10},{9,11},{10,... | collective-permute-start | bytes 884744 | tf_op jit(solution)/shard_map/ppermute | solution.py:198
  13.6 29.1 %collective-permute-start = (bf16[576,768]{1,0:T(8,128)(2,1)}, bf16[576,768]{1,0:T(8,128)(2,1)}, u32[]{:S(2)}, u32[]{:S(2)}) collective-permute-start(bf16[576,768]{1,0:T(8,128)(2,1)} %bitcast.142), channel_id=1, source_target_pairs={{0,2},{1,3},{2,0},{3,1},{4,6},{5,7},{6,4},{7,5},{8,10},{9,11},{10,... | collective-permute-start | bytes 2654216 | tf_op jit(solution)/shard_map/ppermute | solution.py:198
  15.6 76.4 %collective-permute-start.6 = (bf16[768,768]{0,1:T(8,128)(2,1)}, bf16[768,768]{0,1:T(8,128)(2,1)}, u32[]{:S(2)}, u32[]{:S(2)}) collective-permute-start(bf16[768,768]{0,1:T(8,128)(2,1)} %bitcast.138), channel_id=1, source_target_pairs={{0,2},{1,3},{2,0},{3,1},{4,6},{5,7},{6,4},{7,5},{8,10},{9,11},{10,... | collective-permute-start | bytes 3538952 | tf_op jit(solution)/shard_map/ppermute | solution.py:198
  15.7 76.1 %collective-permute-start.8 = (bf16[768,768]{1,0:T(8,128)(2,1)}, bf16[768,768]{1,0:T(8,128)(2,1)S(1)}, u32[]{:S(2)}, u32[]{:S(2)}) collective-permute-start(bf16[768,768]{1,0:T(8,128)(2,1)} %param.35), channel_id=1, source_target_pairs={{0,2},{1,3},{2,0},{3,1},{4,6},{5,7},{6,4},{7,5},{8,10},{9,11},{10,... | collective-permute-start | bytes 3538952 | tf_op jit(solution)/shard_map/ppermute | solution.py:198
  23.1 19.7 %copy-start.13 = (bf16[768,3,192]{0,2,1:T(8,128)(2,1)S(1)}, bf16[768,3,192]{0,2,1:T(8,128)(2,1)}, u32[]{:S(2)}) copy-start(bf16[768,3,192]{0,2,1:T(8,128)(2,1)} %param.27) | copy-start | bytes 2654212
  27.5 17.8 %copy-start.2 = (s32[3,2112,128]{2,1,0:T(8,128)}, s32[3,2112,128]{2,1,0:T(8,128)S(1)}, u32[]{:S(2)}) copy-start(s32[3,2112,128]{2,1,0:T(8,128)S(1)} %ids.1.a_1_.a_3_) | copy-start | bytes 9732100
  27.6 19.3 %copy-start.11 = (bf16[192,768]{1,0:T(8,128)(2,1)S(1)}, bf16[192,768]{1,0:T(8,128)(2,1)}, u32[]{:S(2)}) copy-start(bf16[192,768]{1,0:T(8,128)(2,1)} %param.29) | copy-start | bytes 884740
  27.6 17.7 %collective-permute-start.3 = (f32[2,1920]{1,0:T(2,128)S(1)}, f32[2,1920]{1,0:T(2,128)S(1)}, u32[]{:S(2)}, u32[]{:S(2)}) collective-permute-start(f32[2,1920]{1,0:T(2,128)S(1)} %pad_maximum_fusion.13), channel_id=1, source_target_pairs={{0,1},{1,0},{2,3},{3,2},{4,5},{5,4},{6,7},{7,6},{8,9},{9,8},{10,11... | collective-permute-start | bytes 46088 | tf_op jit(solution)/shard_map/ppermute | solution.py:194
  45.3 46.5 %copy-start.4 = (bf16[768,768]{1,0:T(8,128)(2,1)S(1)}, bf16[768,768]{1,0:T(8,128)(2,1)}, u32[]{:S(2)}) copy-start(bf16[768,768]{1,0:T(8,128)(2,1)} %param.35) | copy-start | bytes 3538948
  45.3 51.6 %collective-permute-start.1 = (bf16[1152,768]{1,0:T(8,128)(2,1)}, bf16[1152,768]{1,0:T(8,128)(2,1)}, u32[]{:S(2)}, u32[]{:S(2)}) collective-permute-start(bf16[1152,768]{1,0:T(8,128)(2,1)} %pad_maximum_fusion.6), channel_id=1, source_target_pairs={{0,1},{1,0},{2,3},{3,2},{4,5},{5,4},{6,7},{7,6},{8,9},{9,8},{10,11... | collective-permute-start | bytes 5308424 | tf_op jit(solution)/shard_map/ppermute | solution.py:194
  46.9 48.6 %collective-permute-start.5 = (bf16[384,768]{1,0:T(8,128)(2,1)S(1)}, bf16[384,768]{1,0:T(8,128)(2,1)S(1)}, u32[]{:S(2)}, u32[]{:S(2)}) collective-permute-start(bf16[384,768]{1,0:T(8,128)(2,1)S(1)} %pad_maximum_fusion.11), channel_id=1, source_target_pairs={{0,1},{1,0},{2,3},{3,2},{4,5},{5,4},{6,7},{7,6},{8,9},{9,8},{10,11... | collective-permute-start | bytes 1769480 | tf_op jit(solution)/shard_map/ppermute | solution.py:194
  48.2 43.8 %copy-start.12 = (bf16[768,768]{1,0:T(8,128)(2,1)S(1)}, bf16[768,768]{1,0:T(8,128)(2,1)}, u32[]{:S(2)}) copy-start(bf16[768,768]{1,0:T(8,128)(2,1)} %param.33) | copy-start | bytes 3538948
  91.9 53.6 %collective-permute-start.9 = (bf16[1536,768]{1,0:T(8,128)(2,1)S(1)}, bf16[1536,768]{1,0:T(8,128)(2,1)S(1)}, u32[]{:S(2)}, u32[]{:S(2)}) collective-permute-start(bf16[1536,768]{1,0:T(8,128)(2,1)S(1)} %pad_maximum_fusion.3), channel_id=1, source_target_pairs={{0,1},{1,0},{2,3},{3,2},{4,5},{5,4},{6,7},{7,6},{8,9},{9,8},{10,11... | collective-permute-start | bytes 7077896 | tf_op jit(solution)/shard_map/ppermute | solution.py:194
  95.0 52.2 %collective-permute-start.7 = (bf16[1536,768]{0,1:T(8,128)(2,1)}, bf16[1536,768]{0,1:T(8,128)(2,1)}, u32[]{:S(2)}, u32[]{:S(2)}) collective-permute-start(bf16[1536,768]{0,1:T(8,128)(2,1)} %pad_maximum_fusion.2), channel_id=1, source_target_pairs={{0,1},{1,0},{2,3},{3,2},{4,5},{5,4},{6,7},{7,6},{8,9},{9,8},{10,11... | collective-permute-start | bytes 7077896 | tf_op jit(solution)/shard_map/ppermute | solution.py:194
  102.4 39.8 %copy-start.24 = (bf16[1,561,768]{2,1,0:T(8,128)(2,1)S(1)}, bf16[1,561,768]{2,1,0:T(8,128)(2,1)}, u32[]{:S(2)}) copy-start(bf16[1,561,768]{2,1,0:T(8,128)(2,1)} %param.26) | copy-start | bytes 2585092
  102.4 39.8 %copy-start.33 = (bf16[768,768]{1,0:T(8,128)(2,1)S(1)}, bf16[768,768]{1,0:T(8,128)(2,1)}, u32[]{:S(2)}) copy-start(bf16[768,768]{1,0:T(8,128)(2,1)} %copy-done.32) | copy-start | bytes 3538948
  102.4 39.8 %copy-start.42 = (f32[768]{0:T(1024)S(1)}, f32[768]{0:T(1024)}, u32[]{:S(2)}) copy-start(f32[768]{0:T(1024)} %param.30) | copy-start | bytes 9220
  167.3 8.2 %copy-start.47 = (bf16[576,3072]{1,0:T(8,128)(2,1)}, bf16[576,3072]{1,0:T(8,128)(2,1)S(1)}, u32[]{:S(2)}) copy-start(bf16[576,3072]{1,0:T(8,128)(2,1)S(1)} %get-tuple-element.145) | copy-start | bytes 10616836
  282.2 48.6 %copy-start.18 = (bf16[576,768]{1,0:T(8,128)(2,1)S(1)}, bf16[576,768]{1,0:T(8,128)(2,1)}, u32[]{:S(2)}) copy-start(bf16[576,768]{1,0:T(8,128)(2,1)} %copy-done.16) | copy-start | bytes 2654212
  283.4 52.5 %collective-permute-start.17 = (bf16[768,384]{0,1:T(8,128)(2,1)}, bf16[768,384]{0,1:T(8,128)(2,1)S(1)}, u32[]{:S(2)}, u32[]{:S(2)}) collective-permute-start(bf16[768,384]{0,1:T(8,128)(2,1)} %convolution_convert_fusion.4), channel_id=1, source_target_pairs={{0,1},{1,0},{2,3},{3,2},{4,5},{5,4},{6,7},{7,6},{8,9},{9,8},{10,11... | collective-permute-start | bytes 1769480 | tf_op jit(solution)/shard_map/ppermute | solution.py:194
  284.2 85.0 %collective-permute-start.10 = (bf16[768,1152]{0,1:T(8,128)(2,1)}, bf16[768,1152]{0,1:T(8,128)(2,1)}, u32[]{:S(2)}, u32[]{:S(2)}) collective-permute-start(bf16[768,1152]{0,1:T(8,128)(2,1)} %convolution_convert_fusion.2), channel_id=1, source_target_pairs={{0,1},{1,0},{2,3},{3,2},{4,5},{5,4},{6,7},{7,6},{8,9},{9,8},{10,11... | collective-permute-start | bytes 5308424 | tf_op jit(solution)/shard_map/ppermute | solution.py:194
  290.0 49.8 %collective-permute-start.15 = (f32[2,1632]{1,0:T(2,128)S(1)}, f32[2,1632]{1,0:T(2,128)S(1)}, u32[]{:S(2)}, u32[]{:S(2)}) collective-permute-start(f32[2,1632]{1,0:T(2,128)S(1)} %slice.311), channel_id=1, source_target_pairs={{0,1},{1,0},{2,3},{3,2},{4,5},{5,4},{6,7},{7,6},{8,9},{9,8},{10,11... | collective-permute-start | bytes 39176 | tf_op jit(solution)/shard_map/ppermute | solution.py:194
  290.5 102.2 %collective-permute-start.27 = (bf16[768,1536]{1,0:T(8,128)(2,1)}, bf16[768,1536]{1,0:T(8,128)(2,1)}, u32[]{:S(2)}, u32[]{:S(2)}) collective-permute-start(bf16[768,1536]{1,0:T(8,128)(2,1)} %convolution_convert_fusion), channel_id=1, source_target_pairs={{0,1},{1,0},{2,3},{3,2},{4,5},{5,4},{6,7},{7,6},{8,9},{9,8},{10,11... | collective-permute-start | bytes 7077896 | tf_op jit(solution)/shard_map/ppermute | solution.py:194
  337.6 29.7 %collective-permute-start.18 = (bf16[768,192]{0,1:T(8,128)(2,1)S(1)}, bf16[768,192]{0,1:T(8,128)(2,1)S(1)}, u32[]{:S(2)}, u32[]{:S(2)}) collective-permute-start(bf16[768,192]{0,1:T(8,128)(2,1)S(1)} %add_convert_fusion.7), channel_id=1, source_target_pairs={{0,2},{1,3},{2,0},{3,1},{4,6},{5,7},{6,4},{7,5},{8,10},{9,11},{10,... | collective-permute-start | bytes 884744 | tf_op jit(solution)/shard_map/ppermute | solution.py:198
  339.9 6.2 %collective-permute-start.16 = (f32[1632]{0:T(1024)S(1)}, f32[1632]{0:T(1024)S(1)}, u32[]{:S(2)}, u32[]{:S(2)}) collective-permute-start(f32[1632]{0:T(1024)S(1)} %get-tuple-element.118), channel_id=1, source_target_pairs={{0,2},{1,3},{2,0},{3,1},{4,6},{5,7},{6,4},{7,5},{8,10},{9,11},{10,... | collective-permute-start | bytes 19592 | tf_op jit(solution)/shard_map/ppermute | solution.py:198
  340.7 56.1 %collective-permute-start.22 = (bf16[768,1536]{1,0:T(8,128)(2,1)}, bf16[768,1536]{1,0:T(8,128)(2,1)}, u32[]{:S(2)}, u32[]{:S(2)}) collective-permute-start(bf16[768,1536]{1,0:T(8,128)(2,1)} %convolution_convert_fusion.1), channel_id=1, source_target_pairs={{0,1},{1,0},{2,3},{3,2},{4,5},{5,4},{6,7},{7,6},{8,9},{9,8},{10,11... | collective-permute-start | bytes 7077896 | tf_op jit(solution)/shard_map/ppermute | solution.py:194
  369.1 6.1 %collective-permute-start.19 = (bf16[4,96,192]{2,1,0:T(8,128)(2,1)S(1)}, bf16[4,96,192]{2,1,0:T(8,128)(2,1)}, u32[]{:S(2)}, u32[]{:S(2)}) collective-permute-start(bf16[4,96,192]{2,1,0:T(8,128)(2,1)S(1)} %bitcast.153), channel_id=1, source_target_pairs={{0,4},{4,0},{8,12},{12,8},{16,20},{20,16},{24,28},{28,24},{1,5},{5... | collective-permute-start | bytes 442376 | tf_op jit(solution)/shard_map/ppermute | solution.py:217
  372.8 16.0 %copy-start.3 = (f32[768,576]{0,1:T(8,128)S(1)}, f32[768,576]{0,1:T(8,128)}, u32[]{:S(2)}) copy-start(f32[768,576]{0,1:T(8,128)} %fusion.44) | copy-start | bytes 5308420
  372.8 16.0 %collective-permute-start.11 = (bf16[768,576]{0,1:T(8,128)(2,1)}, bf16[768,576]{0,1:T(8,128)(2,1)S(1)}, u32[]{:S(2)}, u32[]{:S(2)}) collective-permute-start(bf16[768,576]{0,1:T(8,128)(2,1)} %add_convert_fusion.5), channel_id=1, source_target_pairs={{0,2},{1,3},{2,0},{3,1},{4,6},{5,7},{6,4},{7,5},{8,10},{9,11},{10,... | collective-permute-start | bytes 2654216 | tf_op jit(solution)/shard_map/ppermute | solution.py:198
  376.2 4.7 collective-permute-start.20
  381.5 22.7 %collective-permute-start.21 = (bf16[1,96,192]{2,1,0:T(8,128)(2,1)}, bf16[1,96,192]{2,1,0:T(8,128)(2,1)}, u32[]{:S(2)}, u32[]{:S(2)}) collective-permute-start(bf16[1,96,192]{2,1,0:T(8,128)(2,1)} %constant_dynamic-slice_fusion.2), channel_id=1, source_target_pairs={{0,16},{4,20},{8,24},{12,28},{16,0},{20,4},{24,8},{28,12},{1,17},{... | collective-permute-start | bytes 110600 | tf_op jit(solution)/shard_map/ppermute | solution.py:217
  391.0 11.3 %collective-permute-start.12 = (bf16[4,96,576]{2,1,0:T(8,128)(2,1)S(1)}, bf16[4,96,576]{2,1,0:T(8,128)(2,1)S(1)}, u32[]{:S(2)}, u32[]{:S(2)}) collective-permute-start(bf16[4,96,576]{2,1,0:T(8,128)(2,1)S(1)} %dynamic-slice_bitcast_fusion.2), channel_id=1, source_target_pairs={{0,4},{4,0},{8,12},{12,8},{16,20},{20,16},{24,28},{28,24},{1,5},{5... | collective-permute-start | bytes 1327112 | tf_op jit(solution)/shard_map/ppermute | solution.py:217
  396.5 29.2 %collective-permute-start.28 = (bf16[768,768]{1,0:T(8,128)(2,1)}, bf16[768,768]{1,0:T(8,128)(2,1)}, u32[]{:S(2)}, u32[]{:S(2)}) collective-permute-start(bf16[768,768]{1,0:T(8,128)(2,1)} %add_convert_fusion.1), channel_id=1, source_target_pairs={{0,2},{1,3},{2,0},{3,1},{4,6},{5,7},{6,4},{7,5},{8,10},{9,11},{10,... | collective-permute-start | bytes 3538952 | tf_op jit(solution)/shard_map/ppermute | solution.py:198
  396.7 7.5 %copy-start.28 = (bf16[2,96,192]{2,1,0:T(8,128)(2,1)S(1)}, bf16[2,96,192]{2,1,0:T(8,128)(2,1)}, u32[]{:S(2)}) copy-start(bf16[2,96,192]{2,1,0:T(8,128)(2,1)} %copy-done.27) | copy-start | bytes 221188
  400.5 25.2 %copy-start.10 = (f32[768,768]{1,0:T(8,128)S(1)}, f32[768,768]{1,0:T(8,128)}, u32[]{:S(2)}) copy-start(f32[768,768]{1,0:T(8,128)} %fusion.30) | copy-start | bytes 7077892
  400.5 42.2 %collective-permute-start.23 = (bf16[768,768]{1,0:T(8,128)(2,1)}, bf16[768,768]{1,0:T(8,128)(2,1)}, u32[]{:S(2)}, u32[]{:S(2)}) collective-permute-start(bf16[768,768]{1,0:T(8,128)(2,1)} %add_convert_fusion.3), channel_id=1, source_target_pairs={{0,2},{1,3},{2,0},{3,1},{4,6},{5,7},{6,4},{7,5},{8,10},{9,11},{10,... | collective-permute-start | bytes 3538952 | tf_op jit(solution)/shard_map/ppermute | solution.py:198
  404.1 6.9 %collective-permute-start.13 = (bf16[2,96,576]{2,1,0:T(8,128)(2,1)S(1)}, bf16[2,96,576]{2,1,0:T(8,128)(2,1)S(1)}, u32[]{:S(2)}, u32[]{:S(2)}) collective-permute-start(bf16[2,96,576]{2,1,0:T(8,128)(2,1)S(1)} %dynamic-slice_bitcast_fusion.5), channel_id=1, source_target_pairs={{0,8},{4,12},{8,0},{12,4},{16,24},{20,28},{24,16},{28,20},{1,9},{5... | collective-permute-start | bytes 663560 | tf_op jit(solution)/shard_map/ppermute | solution.py:217
  412.1 34.2 %collective-permute-start.14 = (bf16[1,96,576]{2,1,0:T(8,128)(2,1)S(1)}, bf16[1,96,576]{2,1,0:T(8,128)(2,1)S(1)}, u32[]{:S(2)}, u32[]{:S(2)}) collective-permute-start(bf16[1,96,576]{2,1,0:T(8,128)(2,1)S(1)} %constant_dynamic-slice_fusion.5), channel_id=1, source_target_pairs={{0,16},{4,20},{8,24},{12,28},{16,0},{20,4},{24,8},{28,12},{1,17},{... | collective-permute-start | bytes 331784 | tf_op jit(solution)/shard_map/ppermute | solution.py:217
  425.7 17.0 %copy-start.9 = (f32[768,768]{1,0:T(8,128)S(1)}, f32[768,768]{1,0:T(8,128)}, u32[]{:S(2)}) copy-start(f32[768,768]{1,0:T(8,128)} %fusion.36) | copy-start | bytes 7077892
  427.9 19.5 %collective-permute-start.29 = (bf16[4,96,768]{2,1,0:T(8,128)(2,1)S(1)}, bf16[4,96,768]{2,1,0:T(8,128)(2,1)}, u32[]{:S(2)}, u32[]{:S(2)}) collective-permute-start(bf16[4,96,768]{2,1,0:T(8,128)(2,1)S(1)} %dynamic-slice_bitcast_fusion), channel_id=1, source_target_pairs={{0,4},{4,0},{8,12},{12,8},{16,20},{20,16},{24,28},{28,24},{1,5},{5... | collective-permute-start | bytes 1769480 | tf_op jit(solution)/shard_map/ppermute | solution.py:217
  445.6 10.2 %collective-permute-start.24 = (bf16[4,96,768]{2,1,0:T(8,128)(2,1)}, bf16[4,96,768]{2,1,0:T(8,128)(2,1)}, u32[]{:S(2)}, u32[]{:S(2)}) collective-permute-start(bf16[4,96,768]{2,1,0:T(8,128)(2,1)} %dynamic-slice_bitcast_fusion.1), channel_id=1, source_target_pairs={{0,4},{4,0},{8,12},{12,8},{16,20},{20,16},{24,28},{28,24},{1,5},{5... | collective-permute-start | bytes 1769480 | tf_op jit(solution)/shard_map/ppermute | solution.py:217
  448.6 9.7 %collective-permute-start.30 = (bf16[2,96,768]{2,1,0:T(8,128)(2,1)S(1)}, bf16[2,96,768]{2,1,0:T(8,128)(2,1)S(1)}, u32[]{:S(2)}, u32[]{:S(2)}) collective-permute-start(bf16[2,96,768]{2,1,0:T(8,128)(2,1)S(1)} %dynamic-slice_bitcast_fusion.3), channel_id=1, source_target_pairs={{0,8},{4,12},{8,0},{12,4},{16,24},{20,28},{24,16},{28,20},{1,9},{5... | collective-permute-start | bytes 884744 | tf_op jit(solution)/shard_map/ppermute | solution.py:217
  457.0 17.6 %copy-start.1 = (s32[4,2,561]{2,1,0:T(2,128)S(1)}, s32[4,2,561]{2,1,0:T(2,128)}, u32[]{:S(2)}) copy-start(s32[4,2,561]{2,1,0:T(2,128)} %param.42) | copy-start | bytes 53860
  457.1 9.9 %collective-permute-start.25 = (bf16[2,96,768]{2,1,0:T(8,128)(2,1)S(1)}, bf16[2,96,768]{2,1,0:T(8,128)(2,1)S(1)}, u32[]{:S(2)}, u32[]{:S(2)}) collective-permute-start(bf16[2,96,768]{2,1,0:T(8,128)(2,1)S(1)} %dynamic-slice_bitcast_fusion.4), channel_id=1, source_target_pairs={{0,8},{4,12},{8,0},{12,4},{16,24},{20,28},{24,16},{28,20},{1,9},{5... | collective-permute-start | bytes 884744 | tf_op jit(solution)/shard_map/ppermute | solution.py:217
  458.4 8.8 %collective-permute-start.31 = (bf16[1,96,768]{2,1,0:T(8,128)(2,1)S(1)}, bf16[1,96,768]{2,1,0:T(8,128)(2,1)S(1)}, u32[]{:S(2)}, u32[]{:S(2)}) collective-permute-start(bf16[1,96,768]{2,1,0:T(8,128)(2,1)S(1)} %constant_dynamic-slice_fusion), channel_id=1, source_target_pairs={{0,16},{4,20},{8,24},{12,28},{16,0},{20,4},{24,8},{28,12},{1,17},{... | collective-permute-start | bytes 442376 | tf_op jit(solution)/shard_map/ppermute | solution.py:217
  467.1 6.7 %collective-permute-start.26 = (bf16[1,96,768]{2,1,0:T(8,128)(2,1)S(1)}, bf16[1,96,768]{2,1,0:T(8,128)(2,1)S(1)}, u32[]{:S(2)}, u32[]{:S(2)}) collective-permute-start(bf16[1,96,768]{2,1,0:T(8,128)(2,1)S(1)} %constant_dynamic-slice_fusion.1), channel_id=1, source_target_pairs={{0,16},{4,20},{8,24},{12,28},{16,0},{20,4},{24,8},{28,12},{1,17},{... | collective-permute-start | bytes 442376 | tf_op jit(solution)/shard_map/ppermute | solution.py:217
  (32 other events, 87.5 us)
